TPU v7x, 256 devices: a whole 4x4x8 slice. The times are simulated.
256 devices in a mesh: pair: 2 (over x_lo), ep: 128 (over x_hi, y, z, core).
Axes of the slice: x: 4 (x_hi: 2, x_lo: 2; x = x_hi * 2 + x_lo), y: 4, z: 8, core: 2. Of those that a mesh axis runs over, the one named last changes fastest.
Arguments:
- tokens: bfloat16 [256, 256, 1280], P(('pair', 'ep')), may hold values from -48 to 48
- slot_params: bfloat16 [1280, 128], replicated, may hold values from -1 to 1
- slot_outputs: bfloat16 [256, 128, 1280], P(('pair', 'ep')), may hold values from -1.5 to 1.5
- expert_inputs: bfloat16 [128, 256, 1280], P('ep'), may hold values from -6 to 6
- w_in: bfloat16 [128, 1280, 2560], P('ep', None, 'pair'), may hold values from -0.15625 to 0.15625
- w_out: bfloat16 [128, 2560, 1280], P('ep', 'pair'), may hold values from -0.125 to 0.125
- cotangent: bfloat16 [256, 256, 1280], P(('pair', 'ep')), may hold values from -48 to 48
Outputs:
- d_tokens: bfloat16 [256, 256, 1280], P(('pair', 'ep'))
- d_slot_params: float32 [1280, 128], P(('pair', 'ep'))
- d_w_in: bfloat16 [128, 1280, 2560], P('ep', None, 'pair')
All inputs are finite; a program needn't handle non-finite values.
Results may differ from a plain program's by a relative error of at most 0.011.
Values may be sent and summed in bfloat16 or wider, within the bound.
A program may use at most 64 MiB of HBM per device.

v0:
```python
import jax
import jax.numpy as jnp
from jax import lax
from jax.sharding import PartitionSpec as P


def exact_gelu(value):
    return jax.nn.gelu(value, approximate=False)


def gelu_back(pre, d_act):
    return jax.vjp(exact_gelu, pre)[1](d_act)[0]


def contract(left, right, left_dim, right_dim):
    return lax.dot_general(
        left, right, (((left_dim,), (right_dim,)), ((), ())), preferred_element_type=jnp.float32
    )


def per_device(tokens, slot_params, slot_outputs, expert_inputs, w_in, w_out, cotangent):
    image = tokens[0]
    grad_out = cotangent[0]
    width = image.shape[1]
    logits = jnp.dot(image, slot_params, preferred_element_type=jnp.float32)
    dispatch = jax.nn.softmax(logits, axis=0)
    combine = jax.nn.softmax(logits, axis=1)
    dispatch_b = dispatch.astype(jnp.bfloat16)
    combine_b = combine.astype(jnp.bfloat16)
    d_slot_out = contract(combine_b, grad_out, 0, 0).astype(jnp.bfloat16)
    both = lax.all_gather(d_slot_out[None], "pair", axis=0, tiled=True)
    moved = lax.all_to_all(both, "ep", split_axis=1, concat_axis=1, tiled=True)
    row_grads = moved.reshape(-1, width)
    rows = expert_inputs[0]
    first = w_in[0]
    second = w_out[0]
    pre = jnp.dot(rows, first, preferred_element_type=jnp.float32)
    d_act = contract(row_grads, second, 1, 1)
    d_pre = gelu_back(pre, d_act).astype(jnp.bfloat16)
    d_first = contract(rows, d_pre, 0, 0).astype(jnp.bfloat16)
    summed = lax.psum_scatter(contract(d_pre, first, 1, 1), "pair", scatter_dimension=0, tiled=True)
    back = lax.all_to_all(
        summed.astype(jnp.bfloat16), "ep", split_axis=0, concat_axis=0, tiled=True
    )
    d_disp = contract(image, back, 1, 1)
    d_comb = contract(grad_out, slot_outputs[0], 1, 1)
    d_logits = dispatch * (d_disp - jnp.sum(dispatch * d_disp, axis=0, keepdims=True))
    d_logits = d_logits + combine * (d_comb - jnp.sum(combine * d_comb, axis=1, keepdims=True))
    d_logits_b = d_logits.astype(jnp.bfloat16)
    d_image = jnp.dot(dispatch_b, back, preferred_element_type=jnp.float32) + contract(
        d_logits_b, slot_params, 1, 1
    )
    phi_term = contract(image, d_logits_b, 0, 0)
    d_phi = lax.psum_scatter(phi_term, ("pair", "ep"), scatter_dimension=0, tiled=True)
    return (d_image.astype(jnp.bfloat16)[None], d_phi, d_first[None])


def solution(mesh):
    return jax.shard_map(
        per_device,
        mesh=mesh,
        in_specs=(
            P(("pair", "ep"), None, None),
            P(),
            P(("pair", "ep"), None, None),
            P("ep", None, None),
            P("ep", None, "pair"),
            P("ep", "pair", None),
            P(("pair", "ep"), None, None),
        ),
        out_specs=(P(("pair", "ep"), None, None), P(("pair", "ep"), None), P("ep", None, "pair")),
        check_vma=False,
    )
```

profile of v0, /device:TPU:1, one launch (start us, length us, event | category | flops | bytes accessed | tf_op | source)
XLA Modules:
  0.0 393.7 jit_solution(7887800521055163249)
XLA Ops:
  7.2 1.7 fusion.46
  9.5 8.8 %all-gather = bf16[256,1280]{1,0:T(8,128)(2,1)S(1)} all-gather(bf16[128,1280]{1,0:T(8,128)(2,1)S(1)} %convolution_convert_fusion.1), channel_id=2, replica_groups=mesh['pair'=2,'ep'=128] {'pair'}, dimensions={0}, use_global_device_ids=true | all-gather | bytes 983040 | tf_op jit(solution)/shard_map/all_gather | solution.py:31
  18.4 1.5 copy.22
  19.9 18.1 %all-to-all-start = ((bf16[2,128,1280]{2,0,1:T(2,128)(2,1)}), bf16[2,128,1280]{2,0,1:T(2,128)(2,1)}, u32[]{:S(2)}, u32[]{:S(2)}) async-start(bf16[2,128,1280]{2,0,1:T(2,128)(2,1)} %copy.22), calls=%async_computation | async-start | bytes 1310720 | tf_op jit(solution)/shard_map/all_to_all | solution.py:32
  38.0 3.2 fusion.5
  41.2 19.2 %all-to-all-done = bf16[2,128,1280]{2,0,1:T(2,128)(2,1)} async-done(((bf16[2,128,1280]{2,0,1:T(2,128)(2,1)}), bf16[2,128,1280]{2,0,1:T(2,128)(2,1)}, u32[]{:S(2)}, u32[]{:S(2)}) %all-to-all-start) | async-done | bytes 655392 | tf_op jit(solution)/shard_map/all_to_all | solution.py:32
  60.4 1.3 copy.23
  61.9 5.6 %fusion.13 = bf16[256,1280]{1,0:T(8,128)(2,1)S(1)} fusion(bf16[256,1280]{1,0:T(8,128)(2,1)S(1)} %bitcast.63, bf16[1,1280,1280]{2,1,0:T(8,128)(2,1)} %param.12, f32[256,1280]{1,0:T(8,128)S(1)} %copy-done.10), kind=kOutput, calls=%fused_computation.18 | convolution fusion | flops 862453760 | bytes 5898240 | tf_op jit(solution)/shard_map/dot_general | solution.py:16
  68.3 2.1 fusion.3
  70.4 22.8 %reduce-scatter.3.cloned.1.call-done = f32[128,1280]{1,0:T(8,128)} async-done(((f32[256,1280]{1,0:T(8,128)}), f32[128,1280]{1,0:T(8,128)}) %reduce-scatter.3.cloned.1.call-update) | async-done | bytes 655376 | tf_op jit(solution)/shard_map/reduce_scatter | solution.py:41
  93.2 1.8 convert_bitcast_fusion
  95.6 2.5 reduce
  98.1 1.8 reshape.21
  99.8 14.0 %all-to-all-start.1 = ((bf16[128,2,640]{2,1,0:T(2,128)(2,1)}), bf16[128,2,640]{2,1,0:T(2,128)(2,1)}, u32[]{:S(2)}, u32[]{:S(2)}) async-start(bf16[128,2,640]{2,1,0:T(2,128)(2,1)} %reshape.21), calls=%async_computation.2 | async-start | bytes 655360 | tf_op jit(solution)/shard_map/all_to_all | solution.py:42
  114.1 1.5 fusion.23
  115.6 4.0 %fusion = bf16[1,1280,1280]{1,2,0:T(8,128)(2,1)} fusion(bf16[256,1280]{1,0:T(8,128)(2,1)} %copy-done.11, bf16[1,256,1280]{2,1,0:T(8,128)(2,1)} %param.10), kind=kOutput, calls=%fused_computation.1 | convolution fusion | flops 840499200 | bytes 4587520 | tf_op jit(solution)/shard_map/dot_general | solution.py:16
  119.6 5.6 %copy.29 = bf16[1,1280,1280]{2,1,0:T(8,128)(2,1)} copy(bf16[1,1280,1280]{1,2,0:T(8,128)(2,1)} %fusion) | data formatting | bytes 6553600
  125.3 4.3 %all-to-all-done.1 = bf16[128,2,640]{2,1,0:T(2,128)(2,1)} async-done(((bf16[128,2,640]{2,1,0:T(2,128)(2,1)}), bf16[128,2,640]{2,1,0:T(2,128)(2,1)}, u32[]{:S(2)}, u32[]{:S(2)}) %all-to-all-start.1) | async-done | bytes 327712 | tf_op jit(solution)/shard_map/all_to_all | solution.py:42
  129.5 3.2 reshape.22
  132.7 1.7 multiply_reduce_fusion.1
  135.1 1.3 convolution_bitcast_fusion
  136.5 1.5 fusion.33
  138.0 1.3 fusion.8
  139.3 246.0 %all-reduce.3.cloned.1.call-done = f32[1280,128]{0,1:T(8,128)} async-done(((f32[1280,128]{0,1:T(8,128)}), f32[1280,128]{0,1:T(8,128)}) %all-reduce.3.cloned.1.call-update) | async-done | bytes 655376
  (33 shorter events, 4.8 us)
Async XLA Ops:
  7.2 30.9 %copy-start = (bf16[1,1280,1280]{2,1,0:T(8,128)(2,1)S(1)}, bf16[1,1280,1280]{2,1,0:T(8,128)(2,1)}, u32[]{:S(2)}) copy-start(bf16[1,1280,1280]{2,1,0:T(8,128)(2,1)} %param.11) | copy-start | bytes 9830404
  7.2 1.9 copy-start.2
  19.9 40.5 %all-to-all-start = ((bf16[2,128,1280]{2,0,1:T(2,128)(2,1)}), bf16[2,128,1280]{2,0,1:T(2,128)(2,1)}, u32[]{:S(2)}, u32[]{:S(2)}) async-start(bf16[2,128,1280]{2,0,1:T(2,128)(2,1)} %copy.22), calls=%async_computation | async-start | bytes 1310720 | tf_op jit(solution)/shard_map/all_to_all | solution.py:32
  38.0 55.2 %reduce-scatter.3.cloned.1.call-start = ((), (), s32[]{:S(2)}) async-start(), calls=%async_computation.3 | async-start | bytes 1966080 | tf_op jit(solution)/shard_map/reduce_scatter | solution.py:41
  60.4 1.5 copy-start.10
  67.5 0.8 copy-start.11
  99.8 29.7 %all-to-all-start.1 = ((bf16[128,2,640]{2,1,0:T(2,128)(2,1)}), bf16[128,2,640]{2,1,0:T(2,128)(2,1)}, u32[]{:S(2)}, u32[]{:S(2)}) async-start(bf16[128,2,640]{2,1,0:T(2,128)(2,1)} %reshape.21), calls=%async_computation.2 | async-start | bytes 655360 | tf_op jit(solution)/shard_map/all_to_all | solution.py:42
  113.8 271.4 %all-reduce.3.cloned.1.call-start = ((), (), s32[]{:S(2)}) async-start(), calls=%async_computation.4 | async-start | bytes 1310720
  132.7 2.4 copy-start.1
  134.4 0.6 copy-start.4
  134.5 0.6 copy-start.6
  134.5 0.6 copy-start.8
  136.4 1.5 copy-start.3
  136.4 1.5 copy-start.5
  136.4 1.5 copy-start.7
  136.5 1.5 copy-start.9
Sparse Core Ops, SparseCore 0:
  70.6 22.6 reduce-scatter.2
  136.5 248.6 all-reduce.2
where the time goes:
time: 395 us; the launch traced here: 394 us
  waiting for transfers between devices  292 us (74%)
  starting transfers between devices  32.4 us (8%)
  matrix products  24.2 us (6%)
  local copies, waits for them, and re-layouts  17.3 us (4%)
  between operations  14.2 us (4%)
  blocking collectives  8.82 us (2%)
  other arithmetic  4.51 us (1%)
    unnamed x3, waiting for transfers between devices  246 us
    reduce_scatter x1, waiting for transfers between devices, per_device(): lax.psum_scatter(contract(d_pre, first, 1, 1), 'pair', scatter_dimension=...  22.8 us
    all_to_all x1, waiting for transfers between devices, per_device(): moved = lax.all_to_all(both, 'ep', split_axis=1, concat_axis=1, tiled=True)  19.2 us
    all_to_all x1, starting transfers between devices, per_device(): moved = lax.all_to_all(both, 'ep', split_axis=1, concat_axis=1, tiled=True)  18.1 us
    dot_general x8, matrix products, contract(): lax.dot_general(left, right, (((left_dim,), (right_dim,)), ((), ())), pre...  17.9 us
    unnamed x29, local copies, waits for them, and re-layouts  14.1 us
    all_to_all x1, starting transfers between devices, per_device(): lax.all_to_all(summed.astype(jnp.bfloat16), 'ep', split_axis=0, concat_ax...  14 us
    all_gather x1, blocking collectives, per_device(): both = lax.all_gather(d_slot_out[None], 'pair', axis=0, tiled=True)  8.82 us
  transfers between devices with their start and end apart: 4, of which 4 were waited for; matrix products, arithmetic and copies ran while one was open for 4% of the time, Pallas kernels for 0%

commit v1 on v0

v1 whole, which is shorter than its diff:
```python
import functools

import jax
import jax.numpy as jnp
from jax import lax
from jax.experimental import pallas as pl
from jax.experimental.pallas import tpu as pltpu
from jax.sharding import PartitionSpec as P

F32 = jnp.float32
BF16 = jnp.bfloat16
MESH = pl.DeviceIdType.MESH

NX, NY, NZ, NC = 2, 4, 8, 2
NYC = NY * NC
PLANE = NY * NZ * NC
SLOTS = NX * PLANE
CHUNKS = 5
VMEM_LIMIT = 56 * 2**20

Z1, Y1, N1, P1, R1, P2, N2, Y2, Z2, SC, SY, SX, SF = range(13)


def dot_nn(a, b):
    return lax.dot_general(a, b, (((1,), (0,)), ((), ())), preferred_element_type=F32)


def dot_nt(a, b):
    return lax.dot_general(a, b, (((1,), (1,)), ((), ())), preferred_element_type=F32)


def dot_tn(a, b):
    return lax.dot_general(a, b, (((0,), (0,)), ((), ())), preferred_element_type=F32)


def log2(n):
    return n.bit_length() - 1


def digits(value, sizes):
    out = []
    for size in reversed(sizes):
        out.append(value & (size - 1))
        value = value >> log2(size)
    return out[::-1]


def number(values, sizes):
    total = None
    for value, size in zip(values, sizes):
        total = value if total is None else (total << log2(size)) + value
    return total


def one_hot(source, along):
    r = lax.broadcasted_iota(jnp.int32, (SLOTS, SLOTS), along)
    other = lax.broadcasted_iota(jnp.int32, (SLOTS, SLOTS), 1 - along)
    return jnp.where(source(r) == other, 1.0, 0.0).astype(BF16)


def slot_of_place(r):
    z, h, y, c = digits(r, (NZ, NX, NY, NC))
    return number((h, y, z, c), (NX, NY, NZ, NC))


def turn_source(r):
    yc, h, z = digits(r, (NYC, NX, NZ))
    return number((z, h, yc), (NZ, NX, NYC))


def unturn_source(r):
    z, h, yc = digits(r, (NZ, NX, NYC))
    return number((yc, h, z), (NYC, NX, NZ))


def gather_source(r):
    h, y, z, c = digits(r, (NX, NY, NZ, NC))
    return number((y, c, h, z), (NY, NC, NX, NZ))


def permute(matrix, rows):
    return dot_nn(matrix, rows).astype(BF16)


def kernel(
    tok_h, phi_h, so_h, ei_h, win_h, wout_h, cot_h,
    dtok_h, dphi_o, dwin_h,
    tok, phi, so, ei, win, wout, cot,
    phip, sop, gate, act, dpre, disp, comb, dcomb,
    place, turn, unturn, gath,
    sendz, recvz, sendy, recvy, sendn, rows,
    part, sendp, recvp, sumn, both, sendy2, recvy2, sendz2, back,
    dtok, dwin, ddisp, dlog,
    ph, recvc, sumc, sends, recvs, sumy, recvx, sendf, recvf,
    send_sem, recv_sem, load_sem, out_sem,
):
    wide = tok.shape[1]
    cols = wide // CHUNKS
    hid = win.shape[1]
    hcols = hid // CHUNKS
    fine = wide // (2 * SLOTS)
    zrows = NX * NYC
    yrows = NX * NZ

    p = lax.axis_index("pair")
    e = lax.axis_index("ep")
    c = lax.rem(e, NC)
    z = lax.rem(lax.div(e, NC), NZ)
    y = lax.rem(lax.div(e, NC * NZ), NY)
    h = lax.div(e, PLANE)
    yc = y * NC + c

    def at(pair=p, h=h, y=y, z=z, c=c):
        return (pair, h * PLANE + y * (NZ * NC) + z * NC + c)

    partner = at(pair=1 - p)
    near = at(pair=1 - p, h=1 - h)
    far = at(h=1 - h)
    z_peers = []
    for k in range(1, NZ):
        other = lax.rem(z + k, NZ)
        z_peers.append((other, at(z=other)))
    yc_peers = []
    for k in range(1, NYC):
        other = lax.rem(yc + k, NYC)
        yc_peers.append((other, at(y=lax.div(other, NC), c=lax.rem(other, NC))))
    half = lax.div(z, NZ // 2)
    mine = jnp.logical_and(c == p, half == p)

    def remote(src, dst, step, ch, device):
        return pltpu.make_async_remote_copy(
            src_ref=src, dst_ref=dst, send_sem=send_sem.at[step, ch], recv_sem=recv_sem.at[step, ch],
            device_id=device, device_id_type=MESH,
        )

    def arrived(dst, step, ch):
        pltpu.make_async_copy(dst, dst, recv_sem.at[step, ch]).wait()

    def left(src, step, ch):
        pltpu.make_async_copy(src, src, send_sem.at[step, ch]).wait()

    def aligned(start, size):
        return pl.ds(pl.multiple_of(start, size), size)

    loads = [
        pltpu.make_async_copy(src, dst, load_sem.at[k])
        for k, (src, dst) in enumerate(
            [(tok_h, tok), (phi_h, phi), (cot_h, cot), (ei_h, ei), (win_h, win), (so_h, so), (wout_h, wout)]
        )
    ]
    for load in loads:
        load.start()
    load_tok, load_phi, load_cot, load_ei, load_win, load_so, load_wout = loads

    barrier = pltpu.get_barrier_semaphore()
    for device in [q[1] for q in z_peers] + [q[1] for q in yc_peers] + [partner, near, far]:
        pl.semaphore_signal(barrier, inc=1, device_id=device, device_id_type=MESH)
    for k in range(NZ):
        source = at(pair=half, z=k, c=p)

        @pl.when(jnp.logical_not(jnp.logical_and(mine, z == k)))
        def _():
            pl.semaphore_signal(barrier, inc=1, device_id=source, device_id_type=MESH)

    place[...] = one_hot(slot_of_place, 1)
    turn[...] = one_hot(turn_source, 0)
    unturn[...] = one_hot(unturn_source, 0)
    gath[...] = one_hot(gather_source, 0)

    load_phi.wait()
    phip[...] = dot_nn(phi[...], place[...]).astype(BF16)
    load_tok.wait()
    logits = dot_nn(tok[...], phip[...])
    over_tokens = jnp.exp(logits - jnp.max(logits, axis=0, keepdims=True))
    disp[...] = over_tokens / jnp.sum(over_tokens, axis=0, keepdims=True)
    over_slots = jnp.exp(logits - jnp.max(logits, axis=1, keepdims=True))
    combine = over_slots / jnp.sum(over_slots, axis=1, keepdims=True)
    comb[...] = combine
    combine_t = jnp.transpose(combine).astype(BF16)
    load_cot.wait()

    pl.semaphore_wait(barrier, (NZ - 1) + (NYC - 1) + 3 + NZ - jnp.where(mine, 1, 0))

    for ch in range(CHUNKS):
        sendz[ch] = dot_nn(combine_t, cot[:, ch * cols : (ch + 1) * cols]).astype(BF16)
        for other, device in z_peers:
            remote(sendz.at[ch, aligned(other * zrows, zrows)], recvz.at[ch, aligned(z * zrows, zrows)], Z1, ch, device).start()
        own = aligned(z * zrows, zrows)
        recvz[ch, own, :] = sendz[ch, own, :]

    act[...] = jnp.zeros_like(act)
    load_ei.wait()
    load_win.wait()

    def pre_part(ch):
        span = aligned(ch * hcols, hcols)
        pre = dot_nn(ei[...], win[:, span])
        cdf = 0.5 * (1.0 + lax.erf(pre * (0.5**0.5)))
        pdf = jnp.exp(-0.5 * pre * pre) * 0.3989422804014327
        gate[:, span] = cdf + pre * pdf

    def z_arrives(ch):
        arrived(recvz.at[ch, pl.ds(0, SLOTS - zrows)], Z1, ch)
        sendy[ch] = permute(turn[...], recvz[ch])
        for other, device in yc_peers:
            remote(sendy.at[ch, aligned(other * yrows, yrows)], recvy.at[ch, aligned(yc * yrows, yrows)], Y1, ch, device).start()
        own = aligned(yc * yrows, yrows)
        recvy[ch, own, :] = sendy[ch, own, :]

    here = aligned((p * NX + h) * PLANE, PLANE)
    there = aligned(((1 - p) * NX + 1 - h) * PLANE, PLANE)

    def y_arrives(ch):
        arrived(recvy.at[ch, pl.ds(0, SLOTS - yrows)], Y1, ch)
        sendn[ch] = permute(gath[...], recvy[ch])
        own = sendn.at[ch, aligned(h * PLANE, PLANE)]
        remote(sendn.at[ch, aligned((1 - h) * PLANE, PLANE)], rows.at[ch, here], N1, ch, near).start()
        remote(own, rows.at[ch, here], P1, ch, partner).start()
        rows[ch, here, :] = sendn[ch, aligned(h * PLANE, PLANE), :]

    def near_arrives(ch):
        arrived(rows.at[ch, there], N1, ch)
        remote(rows.at[ch, there], rows.at[ch, there], R1, ch, partner).start()

    def all_arrived(ch):
        arrived(rows.at[ch, here], P1, ch)
        arrived(rows.at[ch, here], R1, ch)
        for k in range(CHUNKS):
            span = slice(k * hcols, (k + 1) * hcols)
            act[:, span] += dot_nt(rows[ch], wout[span, aligned(ch * cols, cols)])

    def pipeline(steps, n):
        def body(t, _):
            for lag, step in steps:
                pl.when(jnp.logical_and(t >= lag, t < lag + n))(functools.partial(step, t - lag))
            return 0

        lax.fori_loop(0, n + max(lag for lag, _ in steps), body, 0)

    pre_part(0)
    load_wout.wait()
    pipeline([(0, z_arrives), (1, y_arrives), (2, near_arrives), (3, all_arrived), (-1, pre_part)], CHUNKS)
    load_so.wait()
    sop[...] = dot_tn(place[...], so[...]).astype(BF16)
    dcomb[...] = dot_nt(cot[...], sop[...])
    dpre[...] = (act[...] * gate[...]).astype(BF16)

    def rows_back(ch):
        part[ch] = dot_nt(dpre[...], win[aligned(ch * cols, cols), :])
        sendp[ch, 0:PLANE, :] = part[ch, aligned(((1 - p) * NX + h) * PLANE, PLANE), :].astype(BF16)
        sendp[ch, PLANE : 2 * PLANE, :] = part[ch, aligned((p * NX + 1 - h) * PLANE, PLANE), :].astype(BF16)
        remote(sendp.at[ch], recvp.at[ch], P2, ch, partner).start()

    def pair_arrives(ch):
        arrived(recvp.at[ch], P2, ch)
        sumn[ch] = (part[ch, there, :] + recvp[ch, PLANE : 2 * PLANE, :].astype(F32)).astype(BF16)
        remote(sumn.at[ch], both.at[ch, aligned(h * PLANE, PLANE)], N2, ch, near).start()
        both[ch, aligned(h * PLANE, PLANE), :] = (part[ch, here, :] + recvp[ch, 0:PLANE, :].astype(F32)).astype(BF16)

    def sums_arrive(ch):
        arrived(sumn.at[ch], N2, ch)
        sendy2[ch] = dot_tn(gath[...], both[ch]).astype(BF16)
        for other, device in yc_peers:
            remote(sendy2.at[ch, aligned(other * yrows, yrows)], recvy2.at[ch, aligned(yc * yrows, yrows)], Y2, ch, device).start()
        own = aligned(yc * yrows, yrows)
        recvy2[ch, own, :] = sendy2[ch, own, :]

    def y_arrives_back(ch):
        arrived(recvy2.at[ch, pl.ds(0, SLOTS - yrows)], Y2, ch)
        sendz2[ch] = permute(unturn[...], recvy2[ch])
        for other, device in z_peers:
            remote(sendz2.at[ch, aligned(other * zrows, zrows)], back.at[ch, aligned(z * zrows, zrows)], Z2, ch, device).start()
        own = aligned(z * zrows, zrows)
        back[ch, own, :] = sendz2[ch, own, :]

    def z_arrives_back(ch):
        arrived(back.at[ch, pl.ds(0, SLOTS - zrows)], Z2, ch)
        ddisp[...] += dot_nt(tok[:, aligned(ch * cols, cols)], back[ch])

    def dwin_part(ch):
        span = aligned(ch * cols, cols)
        for k in range(CHUNKS):
            wide_span = slice(k * hcols, (k + 1) * hcols)
            dwin[span, wide_span] = dot_tn(ei[:, span], dpre[:, wide_span]).astype(BF16)
        pltpu.make_async_copy(dwin.at[span], dwin_h.at[span], out_sem.at[ch]).start()

    ddisp[...] = jnp.zeros_like(ddisp)
    pipeline(
        [(0, rows_back), (1, pair_arrives), (2, sums_arrive), (3, y_arrives_back), (2, dwin_part), (4, z_arrives_back)], CHUNKS
    )

    d_disp = ddisp[...]
    d_comb = dcomb[...]
    dispatch = disp[...]
    combine = comb[...]
    d_logits = dispatch * (d_disp - jnp.sum(dispatch * d_disp, axis=0, keepdims=True))
    d_logits = d_logits + combine * (d_comb - jnp.sum(combine * d_comb, axis=1, keepdims=True))
    d_logits = d_logits.astype(BF16)
    dlog[...] = d_logits

    in_order = dot_nt(d_logits, place[...]).astype(BF16)
    ph[...] = dot_tn(tok[...], in_order)
    top = wide // 2
    remote(ph.at[aligned((1 - c) * top, top)], recvc, SC, 0, at(c=1 - c)).start()

    dispatch_b = disp[...].astype(BF16)

    def d_tokens(ch, _):
        span = aligned(ch * cols, cols)
        dtok[:, span] = (dot_nn(dispatch_b, back[ch]) + dot_nt(dlog[...], phip[span, :])).astype(BF16)
        return 0

    lax.fori_loop(0, CHUNKS, d_tokens, 0)
    store_dtok = pltpu.make_async_copy(dtok, dtok_h, out_sem.at[CHUNKS])
    store_dtok.start()

    arrived(recvc, SC, 0)
    sumc[...] = ph[aligned(c * top, top), :] + recvc[...]
    q = top // (NX * NY)
    for other in range(NY):
        for k in range(NX):
            start = (k * NY + other) * q
            sends[other, k * q : (k + 1) * q, :] = sumc[start : start + q, :].astype(BF16)
    for k in range(1, NY):
        other = lax.rem(y + k, NY)
        remote(sends.at[other], recvs.at[k - 1], SY, 0, at(y=other)).start()
    arrived(recvs, SY, 0)
    from_y = recvs[0].astype(F32)
    for k in range(1, NY - 1):
        from_y = from_y + recvs[k].astype(F32)
    for k in range(NX):
        sumy[k * q : (k + 1) * q, :] = sumc[aligned((k * NY + y) * q, q), :] + from_y[k * q : (k + 1) * q, :]
    quarter = q // 2
    for k, device, piece in (
        (0, partner, h * 2 + 1 - p),
        (1, near, (1 - h) * 2 + 1 - p),
        (2, far, (1 - h) * 2 + p),
    ):
        remote(sumy.at[aligned(piece * quarter, quarter)], recvx.at[k], SX, 0, device).start()
    arrived(recvx, SX, 0)
    sumx = sumy[aligned((h * 2 + p) * quarter, quarter), :] + recvx[0] + recvx[1] + recvx[2]
    sendf[...] = jnp.zeros_like(sendf)
    for k in range(NZ):
        sendf[k, 0:fine, :] = sumx[k * fine : (k + 1) * fine, :]
    for k in range(NZ):
        zk, ck = k // NC, k % NC
        is_me = jnp.logical_and(mine, jnp.logical_and(z == p * (NZ // 2) + zk, c == ck))

        @pl.when(is_me)
        def _():
            pltpu.make_async_copy(sendf.at[k], recvf.at[z], recv_sem.at[SF, 0]).start()

        @pl.when(jnp.logical_not(is_me))
        def _():
            remote(sendf.at[k], recvf.at[z], SF, 0, at(pair=c, z=p * (NZ // 2) + zk, c=ck)).start()

    arrived(recvf, SF, 0)
    total = recvf[0]
    for k in range(1, NZ):
        total = total + recvf[k]
    dphi_o[...] = total[0:fine, :]

    def sent(ch, _):
        left(sendz.at[ch, pl.ds(0, SLOTS - zrows)], Z1, ch)
        left(sendy.at[ch, pl.ds(0, SLOTS - yrows)], Y1, ch)
        left(rows.at[ch, here], N1, ch)
        left(rows.at[ch, here], P1, ch)
        left(rows.at[ch, there], R1, ch)
        left(sendp.at[ch], P2, ch)
        left(sumn.at[ch], N2, ch)
        left(sendy2.at[ch, pl.ds(0, SLOTS - yrows)], Y2, ch)
        left(sendz2.at[ch, pl.ds(0, SLOTS - zrows)], Z2, ch)
        span = aligned(ch * cols, cols)
        pltpu.make_async_copy(dwin.at[span], dwin_h.at[span], out_sem.at[ch]).wait()
        return 0

    lax.fori_loop(0, CHUNKS, sent, 0)
    left(recvc, SC, 0)
    left(recvs, SY, 0)
    left(recvx, SX, 0)

    @pl.when(mine)
    def _():
        left(sendf.at[pl.ds(0, NZ - 1)], SF, 0)

    @pl.when(jnp.logical_not(mine))
    def _():
        left(sendf, SF, 0)

    store_dtok.wait()


def per_device(tokens, slot_params, slot_outputs, expert_inputs, w_in, w_out, cotangent):
    images, (m, wide), slots, hid = 2 * SLOTS, tokens.shape[1:], SLOTS, w_in.shape[2]
    cols = wide // CHUNKS
    fine = wide // images
    top = wide // 2
    q = top // (NX * NY)
    vmem = pltpu.VMEM
    scratch = [
        vmem((m, wide), BF16), vmem((wide, slots), BF16), vmem((slots, wide), BF16), vmem((images, wide), BF16),
        vmem((wide, hid), BF16), vmem((hid, wide), BF16), vmem((m, wide), BF16),
        vmem((wide, slots), BF16), vmem((slots, wide), BF16), vmem((images, hid), F32), vmem((images, hid), F32),
        vmem((images, hid), BF16), vmem((m, slots), F32), vmem((m, slots), F32), vmem((m, slots), F32),
        vmem((slots, slots), BF16), vmem((slots, slots), BF16), vmem((slots, slots), BF16), vmem((slots, slots), BF16),
    ]
    block = vmem((CHUNKS, slots, cols), BF16)
    scratch += [block, block, block, block, block, vmem((CHUNKS, images, cols), BF16)]
    scratch += [vmem((CHUNKS, images, cols), F32), block, block, vmem((CHUNKS, PLANE, cols), BF16)]
    scratch += [block, block, block, block, block]
    scratch += [vmem((m, wide), BF16), vmem((wide, hid), BF16), vmem((m, slots), F32), vmem((m, slots), BF16)]
    scratch += [
        vmem((wide, slots), F32), vmem((top, slots), F32), vmem((top, slots), F32),
        vmem((NY, NX * q, slots), BF16), vmem((NY - 1, NX * q, slots), BF16), vmem((NX * q, slots), F32),
        vmem((3, q // 2, slots), F32), vmem((NZ, 8, slots), F32), vmem((NZ, 8, slots), F32),
    ]
    sems = pltpu.SemaphoreType.DMA
    scratch += [sems((13, CHUNKS)), sems((13, CHUNKS)), sems((7,)), sems((CHUNKS + 1,))]
    hbm = pl.BlockSpec(memory_space=pl.ANY)
    d_tokens, d_phi, d_first = pl.pallas_call(
        kernel,
        out_shape=[
            jax.ShapeDtypeStruct((m, wide), BF16),
            jax.ShapeDtypeStruct((fine, slots), F32),
            jax.ShapeDtypeStruct((wide, hid), BF16),
        ],
        in_specs=[hbm] * 7,
        out_specs=[hbm, pl.BlockSpec(memory_space=pltpu.VMEM), hbm],
        scratch_shapes=scratch,
        compiler_params=pltpu.CompilerParams(collective_id=0, has_side_effects=True, vmem_limit_bytes=VMEM_LIMIT),
    )(tokens[0], slot_params, slot_outputs[0], expert_inputs[0], w_in[0], w_out[0], cotangent[0])
    return (d_tokens[None], d_phi, d_first[None])


def solution(mesh):
    return jax.shard_map(
        per_device,
        mesh=mesh,
        in_specs=(
            P(("pair", "ep"), None, None),
            P(),
            P(("pair", "ep"), None, None),
            P("ep", None, None),
            P("ep", None, "pair"),
            P("ep", "pair", None),
            P(("pair", "ep"), None, None),
        ),
        out_specs=(P(("pair", "ep"), None, None), P(("pair", "ep"), None), P("ep", None, "pair")),
        check_vma=False,
    )
```

time: 395 us -> 93 us (0.24)
  waiting for transfers between devices: 292 us -> 0 us
  Pallas kernels: 0 us -> 85.1 us
  starting transfers between devices: 32.4 us -> 0 us
  matrix products: 24.2 us -> 0 us
  between operations: 14.2 us -> 0.64 us
  local copies, waits for them, and re-layouts: 17.3 us -> 7.08 us
  blocking collectives: 8.82 us -> 0 us
  other arithmetic: 4.51 us -> 0 us
    unnamed x3 -> x0, waiting for transfers between devices: 246 us -> none
    pallas_call x0 -> x1, Pallas kernels: none -> 85.1 us  [per_device(): pl.pallas_call(kernel, out_shape=[jax.ShapeDtypeStruct((m, wide), BF16),...]
    all_to_all x2 -> x0, starting transfers between devices: 32.1 us -> none  [the longest x1 18.1 us: per_device(): moved = lax.all_to_all(both, 'ep', split_axis=1, concat_axis=1, tiled=True)]
    dot_general x11 -> x0, matrix products: 24.2 us -> none  [the longest x8 17.9 us: contract(): lax.dot_general(left, right, (((left_dim,), (right_dim,)), ((), ())), pre...]
    all_to_all x2 -> x0, waiting for transfers between devices: 23.4 us -> none  [the longest x1 19.2 us: per_device(): moved = lax.all_to_all(both, 'ep', split_axis=1, concat_axis=1, tiled=True)]
    reduce_scatter x1 -> x0, waiting for transfers between devices: 22.8 us -> none  [per_device(): lax.psum_scatter(contract(d_pre, first, 1, 1), 'pair', scatter_dimension=...]
    all_gather x1 -> x0, blocking collectives: 8.82 us -> none  [per_device(): both = lax.all_gather(d_slot_out[None], 'pair', axis=0, tiled=True)]
    unnamed x29 -> x3, local copies, waits for them, and re-layouts: 14.1 us -> 7.08 us
  transfers between devices with their start and end apart: 4 -> 0, of which waited for: 4 -> 0; matrix products, arithmetic and copies ran while one was open for 4% -> 0% of each run, Pallas kernels for 0% -> 0%
where the time goes in v1:
time: 93 us; the launch traced here: 92.8 us
  Pallas kernels  85.1 us (92%)
  local copies, waits for them, and re-layouts  7.08 us (8%)
    pallas_call x1, Pallas kernels, per_device(): pl.pallas_call(kernel, out_shape=[jax.ShapeDtypeStruct((m, wide), BF16),...  85.1 us
    unnamed x3, local copies, waits for them, and re-layouts  7.08 us

profile of v1, /device:TPU:1, one launch (start us, length us, event | category | flops | bytes accessed | tf_op | source)
XLA Modules:
  0.0 92.8 jit_solution(16244943488320203131)
XLA Ops:
  0.6 85.1 %shard_map.94 = (bf16[256,1280]{1,0:T(8,128)(2,1)}, f32[5,128]{1,0:T(8,128)}, bf16[1280,1280]{1,0:T(8,128)(2,1)}) custom-call(bf16[256,1280]{1,0:T(8,128)(2,1)} %bitcast.11, bf16[1280,128]{1,0:T(8,128)(2,1)} %phi_h.1, bf16[128,1280]{1,0:T(8,128)(2,1)} %bitcast.15, bf16[256,1280]{1,0:T(8,128)(2,1)} %bitcast.12, bf16[1280,1280]{1,0:T(8,128)(2,1)} %bitcast.8, ...), custom_call_target="tpu_custom_call" | custom-call | tf_op jit(solution)/shard_map/pallas_call | solution.py:420
  85.7 2.0 %copy.13 = bf16[1,256,1280]{2,1,0:T(8,128)(2,1)} copy(bf16[1,256,1280]{2,1,0:T(8,128)(2,1)} %bitcast.14) | data formatting | bytes 1310720
  87.7 1.3 %copy.14 = f32[5,128]{1,0:T(8,128)} copy(f32[5,128]{1,0:T(8,128)} %get-tuple-element.13) | data formatting | bytes 5120
  89.0 3.8 %copy.15 = bf16[1,1280,1280]{2,1,0:T(8,128)(2,1)} copy(bf16[1,1280,1280]{2,1,0:T(8,128)(2,1)} %bitcast.10) | data formatting | bytes 6553600

commit v2 on v0

v2 whole, which is shorter than its diff:
```python
import functools

import jax
import jax.numpy as jnp
from jax import lax
from jax.experimental import pallas as pl
from jax.experimental.pallas import tpu as pltpu
from jax.sharding import PartitionSpec as P

F32 = jnp.float32
BF16 = jnp.bfloat16
MESH = pl.DeviceIdType.MESH

NX, NY, NZ, NC = 2, 4, 8, 2
SPOTS = NX * NY * NC
PLANE = NY * NZ * NC
SLOTS = NX * PLANE
CHUNKS = 5
VMEM_LIMIT = 44 * 2**20

Z1, W1, W2, Z2, SW, SZ = range(6)


def dot_nn(a, b):
    return lax.dot_general(a, b, (((1,), (0,)), ((), ())), preferred_element_type=F32)


def dot_nt(a, b):
    return lax.dot_general(a, b, (((1,), (1,)), ((), ())), preferred_element_type=F32)


def dot_tn(a, b):
    return lax.dot_general(a, b, (((0,), (0,)), ((), ())), preferred_element_type=F32)


def log2(n):
    return n.bit_length() - 1


def digits(value, sizes):
    out = []
    for size in reversed(sizes[1:]):
        out.append(value & (size - 1))
        value = value >> log2(size)
    out.append(value)
    return out[::-1]


def number(values, sizes):
    total = None
    for value, size in zip(values, sizes):
        total = value if total is None else (total << log2(size)) + value
    return total


def one_hot(source, along, n):
    r = lax.broadcasted_iota(jnp.int32, (n, n), along)
    other = lax.broadcasted_iota(jnp.int32, (n, n), 1 - along)
    return jnp.where(source(r) == other, 1.0, 0.0).astype(BF16)


def slot_of_place(r):
    z, h, y, c = digits(r, (NZ, NX, NY, NC))
    return number((h, y, z, c), (NX, NY, NZ, NC))


def turn_source(r):
    spot, z = digits(r, (SPOTS, NZ))
    return number((z, spot), (NZ, SPOTS))


def image_source(r):
    xy, c, z = digits(r, (2 * NX * NY, NC, NZ))
    return number((xy, z, c), (2 * NX * NY, NZ, NC))


def column_source(fine, r):
    g = (r * (-(-(2**18) // fine))) >> 18
    xy, c, z = digits(g, (2 * NX * NY, NC, NZ))
    return number((xy, z, c), (2 * NX * NY, NZ, NC)) * fine + (r - g * fine)


def kernel(
    tok_h, phi_h, so_h, ei_h, win_h, wout_h, cot_h,
    dtok_o, dphi_o, dwin_o,
    tok, phi, so, ei, win, wout, cot,
    phip, sop, eiq, tokq, gate, act, dpre, disp, comb, dcomb,
    place, turn, sort,
    sendz, recvz, sendw, rows, sendw2, recvw2, sendz2, back,
    ddisp, dlog, senda, recva, sendb, recvb,
    send_sem, recv_sem, load_sem,
):
    wide = tok.shape[1]
    cols = wide // CHUNKS
    hid = win.shape[1]
    hcols = hid // CHUNKS
    fine = wide // (2 * SLOTS)
    half = wide // 2

    p = lax.axis_index("pair")
    e = lax.axis_index("ep")
    c = lax.rem(e, NC)
    z = lax.rem(lax.div(e, NC), NZ)
    y = lax.rem(lax.div(e, NC * NZ), NY)
    h = lax.div(e, PLANE)
    spot = (h * NY + y) * NC + c
    me = p * SPOTS + spot

    z_peers = []
    for k in (NZ // 2, *(j for i in range(NZ // 2 - 1, 0, -1) for j in (i, NZ - i))):
        other = lax.rem(z + k, NZ)
        z_peers.append((other, (p, h * PLANE + y * (NZ * NC) + other * NC + c)))
    w_peers = []
    for dy in (NY // 2, *(j for i in range(NY // 2 - 1, 0, -1) for j in (i, NY - i)), 0):
        for dh, dp in ((1, 0), (1, 1), (0, 1), (0, 0)):
            for dc in range(NC - 1, -1, -1):
                if (dy, dh, dp, dc) == (0, 0, 0, 0):
                    continue
                h2, y2, c2, p2 = lax.rem(h + dh, NX), lax.rem(y + dy, NY), lax.rem(c + dc, NC), lax.rem(p + dp, 2)
                spot2 = (h2 * NY + y2) * NC + c2
                w_peers.append((spot2, p2 * SPOTS + spot2, (p2, h2 * PLANE + y2 * (NZ * NC) + z * NC + c2)))

    def send(src, dst, step, ch, device):
        pltpu.make_async_remote_copy(
            src_ref=src, dst_ref=dst, send_sem=send_sem.at[step, ch], recv_sem=recv_sem.at[step, ch],
            device_id=device, device_id_type=MESH,
        ).start()

    def arrived(dst, step, ch):
        pltpu.make_async_copy(dst, dst, recv_sem.at[step, ch]).wait()

    def left(src, step, ch):
        pltpu.make_async_copy(src, src, send_sem.at[step, ch]).wait()

    def aligned(start, size):
        return pl.ds(pl.multiple_of(start, size), size)

    loads = [
        pltpu.make_async_copy(src, dst, load_sem.at[k])
        for k, (src, dst) in enumerate(
            [(tok_h, tok), (phi_h, phi), (cot_h, cot), (ei_h, ei), (win_h, win), (wout_h, wout), (so_h, so)]
        )
    ]
    for load in loads:
        load.start()
    load_tok, load_phi, load_cot, load_ei, load_win, load_wout, load_so = loads

    barrier = pltpu.get_barrier_semaphore()
    for peer in z_peers + w_peers:
        pl.semaphore_signal(barrier, inc=1, device_id=peer[-1], device_id_type=MESH)

    place[...] = one_hot(slot_of_place, 1, SLOTS)
    turn[...] = one_hot(turn_source, 0, SLOTS)

    load_phi.wait()
    phip[...] = dot_nn(phi[...], place[...]).astype(BF16)
    load_tok.wait()
    logits = dot_nn(tok[...], phip[...])
    over_tokens = jnp.exp(logits - jnp.max(logits, axis=0, keepdims=True))
    disp[...] = over_tokens / jnp.sum(over_tokens, axis=0, keepdims=True)
    over_slots = jnp.exp(logits - jnp.max(logits, axis=1, keepdims=True))
    combine = over_slots / jnp.sum(over_slots, axis=1, keepdims=True)
    comb[...] = combine
    combine_t = jnp.transpose(combine).astype(BF16)
    load_cot.wait()

    pl.semaphore_wait(barrier, len(z_peers) + len(w_peers))

    for ch in range(CHUNKS):
        d_slot_out = dot_nn(combine_t, cot[:, ch * cols : (ch + 1) * cols])
        sendz[ch] = d_slot_out.reshape(NZ, SPOTS, cols).astype(BF16)
        for other, device in z_peers:
            send(sendz.at[ch, other], recvz.at[ch, z], Z1, ch, device)
        recvz[ch, z] = sendz[ch, z]

    sort[...] = one_hot(image_source, 0, 2 * SLOTS)
    load_ei.wait()
    eiq[...] = dot_nn(sort[...], ei[...]).astype(BF16)
    load_win.wait()

    def pre_part(ch, _):
        span = aligned(ch * hcols, hcols)
        pre = dot_nn(eiq[...], win[:, span])
        cdf = 0.5 * (1.0 + lax.erf(pre * (0.5**0.5)))
        pdf = jnp.exp(-0.5 * pre * pre) * 0.3989422804014327
        gate[:, span] = cdf + pre * pdf
        return 0

    lax.fori_loop(0, CHUNKS, pre_part, 0)

    def z_arrives(ch, _):
        arrived(recvz.at[ch, pl.ds(0, NZ - 1)], Z1, ch)
        turned = dot_nn(turn[...], recvz[ch].reshape(SLOTS, cols))
        sendw[ch] = turned.reshape(SPOTS, NZ, cols).astype(BF16)
        for other, _, device in w_peers:
            send(sendw.at[ch, other], rows.at[ch, me], W1, ch, device)
        rows[ch, me] = sendw[ch, spot]
        return 0

    lax.fori_loop(0, CHUNKS, z_arrives, 0)
    act[...] = jnp.zeros_like(act)
    load_wout.wait()

    def rows_arrive(ch, _):
        arrived(rows.at[ch, pl.ds(0, 2 * SPOTS - 1)], W1, ch)
        grads = rows[ch].reshape(2 * SLOTS, cols)
        for k in range(CHUNKS):
            span = slice(k * hcols, (k + 1) * hcols)
            act[:, span] += dot_nt(grads, wout[span, aligned(ch * cols, cols)])
        return 0

    lax.fori_loop(0, CHUNKS, rows_arrive, 0)
    dpre[...] = (act[...] * gate[...]).astype(BF16)

    def rows_back(ch, _):
        part = dot_nt(dpre[...], win[aligned(ch * cols, cols), :])
        sendw2[ch] = part.reshape(2 * SPOTS, NZ, cols).astype(BF16)
        for _, other, device in w_peers:
            send(sendw2.at[ch, other], recvw2.at[ch, me], W2, ch, device)
        recvw2[ch, me] = sendw2[ch, me]
        return 0

    lax.fori_loop(0, CHUNKS, rows_back, 0)

    def dwin_part(ch, _):
        span = aligned(ch * cols, cols)
        for k in range(CHUNKS):
            wide_span = slice(k * hcols, (k + 1) * hcols)
            dwin_o[span, wide_span] = dot_tn(eiq[:, span], dpre[:, wide_span]).astype(BF16)
        return 0

    lax.fori_loop(0, CHUNKS, dwin_part, 0)

    def pair_arrives(ch, _):
        arrived(recvw2.at[ch, pl.ds(0, 2 * SPOTS - 1)], W2, ch)
        summed = recvw2[ch, 0:SPOTS].astype(F32) + recvw2[ch, SPOTS : 2 * SPOTS].astype(F32)
        turned = dot_tn(turn[...], summed.reshape(SLOTS, cols).astype(BF16))
        sendz2[ch] = turned.reshape(NZ, SPOTS, cols).astype(BF16)
        for other, device in z_peers:
            send(sendz2.at[ch, other], back.at[ch, z], Z2, ch, device)
        back[ch, z] = sendz2[ch, z]
        return 0

    lax.fori_loop(0, CHUNKS, pair_arrives, 0)

    load_so.wait()
    sop[...] = dot_tn(place[...], so[...]).astype(BF16)
    dcomb[...] = dot_nt(cot[...], sop[...])
    order = one_hot(functools.partial(column_source, fine), 1, half)
    for k in range(2):
        tokq[:, k * half : (k + 1) * half] = dot_nn(tok[:, k * half : (k + 1) * half], order).astype(BF16)
    ddisp[...] = jnp.zeros_like(ddisp)

    def z_arrives_back(ch, _):
        arrived(back.at[ch, pl.ds(0, NZ - 1)], Z2, ch)
        ddisp[...] += dot_nt(tok[:, aligned(ch * cols, cols)], back[ch].reshape(SLOTS, cols))
        return 0

    lax.fori_loop(0, CHUNKS, z_arrives_back, 0)

    d_disp = ddisp[...]
    d_comb = dcomb[...]
    dispatch = disp[...]
    combine = comb[...]
    d_logits = dispatch * (d_disp - jnp.sum(dispatch * d_disp, axis=0, keepdims=True))
    d_logits = d_logits + combine * (d_comb - jnp.sum(combine * d_comb, axis=1, keepdims=True))
    d_logits = d_logits.astype(BF16)
    dlog[...] = d_logits

    in_order = dot_nt(d_logits, place[...]).astype(BF16)
    senda[...] = dot_tn(tokq[...], in_order).reshape(2 * SPOTS, NZ * fine, SLOTS).astype(BF16)
    for _, other, device in w_peers:
        send(senda.at[other], recva.at[me], SW, 0, device)
    recva[me] = senda[me]

    dispatch_b = disp[...].astype(BF16)

    def d_tokens(ch, _):
        span = aligned(ch * cols, cols)
        dtok_o[:, span] = (
            dot_nn(dispatch_b, back[ch].reshape(SLOTS, cols)) + dot_nt(dlog[...], phip[span, :])
        ).astype(BF16)
        return 0

    lax.fori_loop(0, CHUNKS, d_tokens, 0)

    arrived(recva.at[pl.ds(0, 2 * SPOTS - 1)], SW, 0)
    summed = recva[0].astype(F32)
    for k in range(1, 2 * SPOTS):
        summed = summed + recva[k].astype(F32)
    sendb[...] = jnp.zeros_like(sendb)
    for k in range(NZ):
        sendb[k, 0:fine, :] = summed[k * fine : (k + 1) * fine, :]
    for other, device in z_peers:
        send(sendb.at[other], recvb.at[z], SZ, 0, device)
    recvb[z] = sendb[z]
    arrived(recvb.at[pl.ds(0, NZ - 1)], SZ, 0)
    total = recvb[0]
    for k in range(1, NZ):
        total = total + recvb[k]
    dphi_o[...] = total[0:fine, :]

    def sent(ch, _):
        left(sendz.at[ch, pl.ds(0, NZ - 1)], Z1, ch)
        left(rows.at[ch, pl.ds(0, 2 * SPOTS - 1)], W1, ch)
        left(sendw2.at[ch, pl.ds(0, 2 * SPOTS - 1)], W2, ch)
        left(sendz2.at[ch, pl.ds(0, NZ - 1)], Z2, ch)
        return 0

    lax.fori_loop(0, CHUNKS, sent, 0)
    left(senda.at[pl.ds(0, 2 * SPOTS - 1)], SW, 0)
    left(sendb.at[pl.ds(0, NZ - 1)], SZ, 0)


def write_out(dtok_i, dphi_i, dwin_i, dtok_o, dphi_o, dwin_o, sem):
    copies = [
        pltpu.make_async_copy(src, dst, sem.at[k])
        for k, (src, dst) in enumerate([(dwin_i, dwin_o), (dtok_i, dtok_o), (dphi_i, dphi_o)])
    ]
    for copy in copies:
        copy.start()
    for copy in copies:
        copy.wait()


def per_device(tokens, slot_params, slot_outputs, expert_inputs, w_in, w_out, cotangent):
    images, (m, wide), slots, hid = 2 * SLOTS, tokens.shape[1:], SLOTS, w_in.shape[2]
    cols = wide // CHUNKS
    fine = wide // images
    vmem = pltpu.VMEM
    scratch = [
        vmem((m, wide), BF16), vmem((wide, slots), BF16), vmem((slots, wide), BF16), vmem((images, wide), BF16),
        vmem((wide, hid), BF16), vmem((hid, wide), BF16), vmem((m, wide), BF16),
        vmem((wide, slots), BF16), vmem((slots, wide), BF16), vmem((images, wide), BF16), vmem((m, wide), BF16),
        vmem((images, hid), F32), vmem((images, hid), F32),
        vmem((images, hid), BF16), vmem((m, slots), F32), vmem((m, slots), F32), vmem((m, slots), F32),
        vmem((slots, slots), BF16), vmem((slots, slots), BF16), vmem((images, images), BF16),
    ]
    by_z = vmem((CHUNKS, NZ, SPOTS, cols), BF16)
    by_spot = vmem((CHUNKS, SPOTS, NZ, cols), BF16)
    by_device = vmem((CHUNKS, 2 * SPOTS, NZ, cols), BF16)
    scratch += [by_z, by_z, by_spot, by_device, by_device, by_device, by_z, by_z]
    scratch += [
        vmem((m, slots), F32), vmem((m, slots), BF16),
        vmem((2 * SPOTS, NZ * fine, slots), BF16), vmem((2 * SPOTS, NZ * fine, slots), BF16),
        vmem((NZ, 8, slots), F32), vmem((NZ, 8, slots), F32),
    ]
    sems = pltpu.SemaphoreType.DMA
    scratch += [sems((6, CHUNKS)), sems((6, CHUNKS)), sems((7,))]
    hbm = pl.BlockSpec(memory_space=pl.ANY)
    held = pl.BlockSpec(memory_space=pltpu.VMEM)
    shapes = [
        jax.ShapeDtypeStruct((m, wide), BF16),
        jax.ShapeDtypeStruct((fine, slots), F32),
        jax.ShapeDtypeStruct((wide, hid), BF16),
    ]
    args = (tokens[0], slot_params, slot_outputs[0], expert_inputs[0], w_in[0], w_out[0], cotangent[0])
    results = pl.pallas_call(
        kernel,
        out_shape=[pltpu.VMEM(shape.shape, shape.dtype) for shape in shapes],
        in_specs=[hbm] * 7,
        out_specs=[held] * 3,
        scratch_shapes=scratch,
        compiler_params=pltpu.CompilerParams(collective_id=0, has_side_effects=True, vmem_limit_bytes=VMEM_LIMIT),
    )(*[pltpu.with_memory_space_constraint(arg, pltpu.HBM) for arg in args])
    d_tokens, d_phi, d_first = pl.pallas_call(
        write_out,
        out_shape=shapes,
        in_specs=[hbm] * 3,
        out_specs=[hbm] * 3,
        scratch_shapes=[sems((3,))],
    )(*results)
    return (d_tokens[None], d_phi, d_first[None])


def solution(mesh):
    return jax.shard_map(
        per_device,
        mesh=mesh,
        in_specs=(
            P(("pair", "ep"), None, None),
            P(),
            P(("pair", "ep"), None, None),
            P("ep", None, None),
            P("ep", None, "pair"),
            P("ep", "pair", None),
            P(("pair", "ep"), None, None),
        ),
        out_specs=(P(("pair", "ep"), None, None), P(("pair", "ep"), None), P("ep", None, "pair")),
        check_vma=False,
    )
```

time: 395 us -> 177 us (0.45)
  waiting for transfers between devices: 292 us -> 0 us
  Pallas kernels: 0 us -> 173 us
  starting transfers between devices: 32.4 us -> 0 us
  matrix products: 24.2 us -> 0 us
  local copies, waits for them, and re-layouts: 17.3 us -> 3.08 us
  between operations: 14.2 us -> 0.65 us
  blocking collectives: 8.82 us -> 0 us
  other arithmetic: 4.51 us -> 0 us
    unnamed x3 -> x0, waiting for transfers between devices: 246 us -> none
    pallas_call x0 -> x2, Pallas kernels: none -> 173 us  [the longest x1 120 us: per_device(): pl.pallas_call(write_out, out_shape=shapes, in_specs=[hbm] * 3, out_specs...]
    all_to_all x2 -> x0, starting transfers between devices: 32.1 us -> none  [the longest x1 18.1 us: per_device(): moved = lax.all_to_all(both, 'ep', split_axis=1, concat_axis=1, tiled=True)]
    dot_general x11 -> x0, matrix products: 24.2 us -> none  [the longest x8 17.9 us: contract(): lax.dot_general(left, right, (((left_dim,), (right_dim,)), ((), ())), pre...]
    all_to_all x2 -> x0, waiting for transfers between devices: 23.4 us -> none  [the longest x1 19.2 us: per_device(): moved = lax.all_to_all(both, 'ep', split_axis=1, concat_axis=1, tiled=True)]
    reduce_scatter x1 -> x0, waiting for transfers between devices: 22.8 us -> none  [per_device(): lax.psum_scatter(contract(d_pre, first, 1, 1), 'pair', scatter_dimension=...]
    unnamed x29 -> x6, local copies, waits for them, and re-layouts: 14.1 us -> 3.08 us
    all_gather x1 -> x0, blocking collectives: 8.82 us -> none  [per_device(): both = lax.all_gather(d_slot_out[None], 'pair', axis=0, tiled=True)]
  transfers between devices with their start and end apart: 4 -> 0, of which waited for: 4 -> 0; matrix products, arithmetic and copies ran while one was open for 4% -> 0% of each run, Pallas kernels for 0% -> 0%
where the time goes in v2:
time: 177 us
  Pallas kernels  173 us (98%)
  local copies, waits for them, and re-layouts  3.08 us (2%)
    pallas_call x1, Pallas kernels, per_device(): pl.pallas_call(write_out, out_shape=shapes, in_specs=[hbm] * 3, out_specs...  120 us
    pallas_call x1, Pallas kernels, per_device(): pl.pallas_call(kernel, out_shape=[pltpu.VMEM(shape.shape, shape.dtype) fo...  53.1 us

profile of v2, /device:TPU:1, one launch (start us, length us, event | category | flops | bytes accessed | tf_op | source)
XLA Modules:
  0.0 177.2 jit_solution(15932735747211105892)
XLA Ops:
  0.6 53.1 %shard_map.94 = (bf16[256,1280]{1,0:T(8,128)(2,1)S(1)}, f32[5,128]{1,0:T(8,128)S(1)}, bf16[1280,1280]{1,0:T(8,128)(2,1)S(1)}) custom-call(bf16[256,1280]{1,0:T(8,128)(2,1)} %bitcast.10, bf16[1280,128]{1,0:T(8,128)(2,1)} %phi_h.1, bf16[128,1280]{1,0:T(8,128)(2,1)} %bitcast.13, bf16[256,1280]{1,0:T(8,128)(2,1)} %bitcast.11, bf16[1280,1280]{1,0:T(8,128)(2,1)} %bitcast.8, ...), custom_call_target="tpu_custom_call" | custom-call | tf_op jit(solution)/shard_map/pallas_call | solution.py:358
  53.8 0.0 copy-start
  53.8 1.7 copy-done
  55.4 0.0 copy-start.1
  55.4 0.8 copy-done.1
  56.3 0.0 copy-start.2
  56.3 0.6 copy-done.2
  56.9 120.3 %shard_map.95 = (bf16[256,1280]{1,0:T(8,128)(2,1)}, f32[5,128]{1,0:T(8,128)}, bf16[1280,1280]{1,0:T(8,128)(2,1)}) custom-call(bf16[256,1280]{1,0:T(8,128)(2,1)} %copy-done.1, f32[5,128]{1,0:T(8,128)} %copy-done.2, bf16[1280,1280]{1,0:T(8,128)(2,1)} %copy-done), custom_call_target="tpu_custom_call" | custom-call | tf_op jit(solution)/shard_map/pallas_call | solution.py:366
Async XLA Ops:
  53.8 1.7 copy-start
  55.4 0.8 copy-start.1
  56.3 0.6 copy-start.2

commit v3 on v2

--- a/solution.py
+++ b/solution.py
@@ -369,7 +369,8 @@
         in_specs=[hbm] * 3,
         out_specs=[hbm] * 3,
         scratch_shapes=[sems((3,))],
-    )(*results)
+        compiler_params=pltpu.CompilerParams(vmem_limit_bytes=2**20),
+    )(*[pltpu.with_memory_space_constraint(result, pltpu.VMEM) for result in results])
     return (d_tokens[None], d_phi, d_first[None])
 
 

time: 177 us -> 55.8 us (0.32)
  Pallas kernels: 173 us -> 55.1 us
  local copies, waits for them, and re-layouts: 3.08 us -> 0 us
    pallas_call x1, Pallas kernels: 120 us -> 1.94 us  [per_device(): pl.pallas_call(write_out, out_shape=shapes, in_specs=[hbm] * 3, out_specs...]
    unnamed x6 -> x0, local copies, waits for them, and re-layouts: 3.08 us -> none
where the time goes in v3:
time: 55.8 us; the launch traced here: 55.7 us
  Pallas kernels  55.1 us (99%)
  between operations  0.64 us (1%)
    pallas_call x1, Pallas kernels, per_device(): pl.pallas_call(kernel, out_shape=[pltpu.VMEM(shape.shape, shape.dtype) fo...  53.1 us
    pallas_call x1, Pallas kernels, per_device(): pl.pallas_call(write_out, out_shape=shapes, in_specs=[hbm] * 3, out_specs...  1.94 us

profile of v3, /device:TPU:1, one launch (start us, length us, event | category | flops | bytes accessed | tf_op | source)
XLA Modules:
  0.0 55.7 jit_solution(8606988707565310280)
XLA Ops:
  0.6 53.1 %shard_map.94 = (bf16[256,1280]{1,0:T(8,128)(2,1)S(1)}, f32[5,128]{1,0:T(8,128)S(1)}, bf16[1280,1280]{1,0:T(8,128)(2,1)S(1)}) custom-call(bf16[256,1280]{1,0:T(8,128)(2,1)} %bitcast.10, bf16[1280,128]{1,0:T(8,128)(2,1)} %phi_h.1, bf16[128,1280]{1,0:T(8,128)(2,1)} %bitcast.13, bf16[256,1280]{1,0:T(8,128)(2,1)} %bitcast.11, bf16[1280,1280]{1,0:T(8,128)(2,1)} %bitcast.8, ...), custom_call_target="tpu_custom_call" | custom-call | tf_op jit(solution)/shard_map/pallas_call | solution.py:358
  53.8 1.9 %shard_map.95 = (bf16[256,1280]{1,0:T(8,128)(2,1)}, f32[5,128]{1,0:T(8,128)}, bf16[1280,1280]{1,0:T(8,128)(2,1)}) custom-call(bf16[256,1280]{1,0:T(8,128)(2,1)S(1)} %get-tuple-element.9.dtok_i, f32[5,128]{1,0:T(8,128)S(1)} %get-tuple-element.10.dphi_i, bf16[1280,1280]{1,0:T(8,128)(2,1)S(1)} %get-tuple-element.11.dwin_i), custom_call_target="tpu_custom_call" | custom-call | tf_op jit(solution)/shard_map/pallas_call | solution.py:366

commit v4 on v3

--- a/solution.py
+++ b/solution.py
@@ -15,10 +15,10 @@
 SPOTS = NX * NY * NC
 PLANE = NY * NZ * NC
 SLOTS = NX * PLANE
-CHUNKS = 5
+TILE = 256
 VMEM_LIMIT = 44 * 2**20
 
-Z1, W1, W2, Z2, SW, SZ = range(6)
+Z1, W1, W2, Z2, V1, M1, M2, V2, SW, SZ = range(10)
 
 
 def dot_nn(a, b):
@@ -69,6 +69,11 @@
     return number((z, spot), (NZ, SPOTS))
 
 
+def swap_source(r):
+    z, device = digits(r, (NZ, 2 * SPOTS))
+    return number((device, z), (2 * SPOTS, NZ))
+
+
 def image_source(r):
     xy, c, z = digits(r, (2 * NX * NY, NC, NZ))
     return number((xy, z, c), (2 * NX * NY, NZ, NC))
@@ -85,15 +90,15 @@
     dtok_o, dphi_o, dwin_o,
     tok, phi, so, ei, win, wout, cot,
     phip, sop, eiq, tokq, gate, act, dpre, disp, comb, dcomb,
-    place, turn, sort,
+    place, turn, sort, swap, combine_s,
     sendz, recvz, sendw, rows, sendw2, recvw2, sendz2, back,
-    ddisp, dlog, senda, recva, sendb, recvb,
+    sendm, recvm, sendm2, recvm2,
+    combine_t, ddisp, dlog, senda, recva, sendb, recvb,
     send_sem, recv_sem, load_sem,
 ):
     wide = tok.shape[1]
-    cols = wide // CHUNKS
     hid = win.shape[1]
-    hcols = hid // CHUNKS
+    pieces = hid // TILE
     fine = wide // (2 * SLOTS)
     half = wide // 2
 
@@ -133,7 +138,31 @@
         pltpu.make_async_copy(src, src, send_sem.at[step, ch]).wait()
 
     def aligned(start, size):
+        if isinstance(start, int):
+            return pl.ds(start, size)
         return pl.ds(pl.multiple_of(start, size), size)
+
+    half_tile = TILE // 2
+    tail = pl.ds(3 * TILE, half_tile)
+    mixed = pl.ds(3 * TILE + half_tile, 3 * half_tile)
+
+    def whole_span(k):
+        return aligned(k * TILE, TILE)
+
+    def mixed_span(k):
+        return aligned((7 + k) * half_tile, half_tile)
+
+    def thrice(*steps):
+        def body(k, _):
+            for step, span_of in steps:
+                step(span_of(k), k)
+            return 0
+
+        lax.fori_loop(0, 3, body, 0)
+
+    barrier = pltpu.get_barrier_semaphore()
+    for peer in z_peers + w_peers:
+        pl.semaphore_signal(barrier, inc=1, device_id=peer[-1], device_id_type=MESH)
 
     loads = [
         pltpu.make_async_copy(src, dst, load_sem.at[k])
@@ -145,12 +174,9 @@
         load.start()
     load_tok, load_phi, load_cot, load_ei, load_win, load_wout, load_so = loads
 
-    barrier = pltpu.get_barrier_semaphore()
-    for peer in z_peers + w_peers:
-        pl.semaphore_signal(barrier, inc=1, device_id=peer[-1], device_id_type=MESH)
-
     place[...] = one_hot(slot_of_place, 1, SLOTS)
     turn[...] = one_hot(turn_source, 0, SLOTS)
+    swap[...] = one_hot(swap_source, 0, 2 * SLOTS)
 
     load_phi.wait()
     phip[...] = dot_nn(phi[...], place[...]).astype(BF16)
@@ -161,102 +187,154 @@
     over_slots = jnp.exp(logits - jnp.max(logits, axis=1, keepdims=True))
     combine = over_slots / jnp.sum(over_slots, axis=1, keepdims=True)
     comb[...] = combine
-    combine_t = jnp.transpose(combine).astype(BF16)
+    combine_t[...] = jnp.transpose(combine).astype(BF16)
+    combine_s[...] = dot_nn(turn[...], combine_t[...]).astype(BF16)
     load_cot.wait()
 
     pl.semaphore_wait(barrier, len(z_peers) + len(w_peers))
 
-    for ch in range(CHUNKS):
-        d_slot_out = dot_nn(combine_t, cot[:, ch * cols : (ch + 1) * cols])
-        sendz[ch] = d_slot_out.reshape(NZ, SPOTS, cols).astype(BF16)
+    def slot_grads(span, k):
+        d_slot_out = dot_nn(combine_t[...], cot[:, span])
+        sendz[:, :, span] = d_slot_out.reshape(NZ, SPOTS, span.size).astype(BF16)
         for other, device in z_peers:
-            send(sendz.at[ch, other], recvz.at[ch, z], Z1, ch, device)
-        recvz[ch, z] = sendz[ch, z]
+            send(sendz.at[other, :, span], recvz.at[z, :, span], Z1, k, device)
+        recvz[z, :, span] = sendz[z, :, span]
+
+    def slot_grads_mixed(span, k):
+        d_slot_out = dot_nn(combine_s[...], cot[:, span])
+        sendw[:, :, span] = d_slot_out.reshape(SPOTS, NZ, span.size).astype(BF16)
+        for other, _, device in w_peers:
+            send(sendw.at[other, :, span], rows.at[me, :, span], V1, k, device)
+        rows[me, :, span] = sendw[spot, :, span]
+
+    thrice((slot_grads, whole_span), (slot_grads_mixed, mixed_span))
+    slot_grads(tail, 3)
 
     sort[...] = one_hot(image_source, 0, 2 * SLOTS)
     load_ei.wait()
     eiq[...] = dot_nn(sort[...], ei[...]).astype(BF16)
     load_win.wait()
 
-    def pre_part(ch, _):
-        span = aligned(ch * hcols, hcols)
+    def pre_part(k, _):
+        span = aligned(k * TILE, TILE)
         pre = dot_nn(eiq[...], win[:, span])
         cdf = 0.5 * (1.0 + lax.erf(pre * (0.5**0.5)))
         pdf = jnp.exp(-0.5 * pre * pre) * 0.3989422804014327
         gate[:, span] = cdf + pre * pdf
         return 0
 
-    lax.fori_loop(0, CHUNKS, pre_part, 0)
-
-    def z_arrives(ch, _):
-        arrived(recvz.at[ch, pl.ds(0, NZ - 1)], Z1, ch)
-        turned = dot_nn(turn[...], recvz[ch].reshape(SLOTS, cols))
-        sendw[ch] = turned.reshape(SPOTS, NZ, cols).astype(BF16)
+    lax.fori_loop(0, pieces, pre_part, 0)
+
+    def z_arrives(span, k):
+        arrived(recvz.at[pl.ds(0, NZ - 1), :, span], Z1, k)
+        turned = dot_nn(turn[...], recvz[:, :, span].reshape(SLOTS, span.size))
+        sendw[:, :, span] = turned.reshape(SPOTS, NZ, span.size).astype(BF16)
         for other, _, device in w_peers:
-            send(sendw.at[ch, other], rows.at[ch, me], W1, ch, device)
-        rows[ch, me] = sendw[ch, spot]
-        return 0
-
-    lax.fori_loop(0, CHUNKS, z_arrives, 0)
+            send(sendw.at[other, :, span], rows.at[me, :, span], W1, k, device)
+        rows[me, :, span] = sendw[spot, :, span]
+
+    def v_arrives(span, k):
+        arrived(rows.at[pl.ds(0, 2 * SPOTS - 1), :, span], V1, k)
+        swapped = dot_nn(swap[...], rows[:, :, span].reshape(2 * SLOTS, span.size))
+        sendm[:, :, span] = swapped.reshape(NZ, 2 * SPOTS, span.size).astype(BF16)
+        for other, device in z_peers:
+            send(sendm.at[other, :, span], recvm.at[z, :, span], M1, k, device)
+        recvm[z, :, span] = sendm[z, :, span]
+
+    thrice((z_arrives, whole_span), (v_arrives, mixed_span))
+    z_arrives(tail, 3)
+
     act[...] = jnp.zeros_like(act)
     load_wout.wait()
-
-    def rows_arrive(ch, _):
-        arrived(rows.at[ch, pl.ds(0, 2 * SPOTS - 1)], W1, ch)
-        grads = rows[ch].reshape(2 * SLOTS, cols)
-        for k in range(CHUNKS):
-            span = slice(k * hcols, (k + 1) * hcols)
-            act[:, span] += dot_nt(grads, wout[span, aligned(ch * cols, cols)])
-        return 0
-
-    lax.fori_loop(0, CHUNKS, rows_arrive, 0)
-    dpre[...] = (act[...] * gate[...]).astype(BF16)
-
-    def rows_back(ch, _):
-        part = dot_nt(dpre[...], win[aligned(ch * cols, cols), :])
-        sendw2[ch] = part.reshape(2 * SPOTS, NZ, cols).astype(BF16)
-        for _, other, device in w_peers:
-            send(sendw2.at[ch, other], recvw2.at[ch, me], W2, ch, device)
-        recvw2[ch, me] = sendw2[ch, me]
-        return 0
-
-    lax.fori_loop(0, CHUNKS, rows_back, 0)
-
-    def dwin_part(ch, _):
-        span = aligned(ch * cols, cols)
-        for k in range(CHUNKS):
-            wide_span = slice(k * hcols, (k + 1) * hcols)
-            dwin_o[span, wide_span] = dot_tn(eiq[:, span], dpre[:, wide_span]).astype(BF16)
-        return 0
-
-    lax.fori_loop(0, CHUNKS, dwin_part, 0)
-
-    def pair_arrives(ch, _):
-        arrived(recvw2.at[ch, pl.ds(0, 2 * SPOTS - 1)], W2, ch)
-        summed = recvw2[ch, 0:SPOTS].astype(F32) + recvw2[ch, SPOTS : 2 * SPOTS].astype(F32)
-        turned = dot_tn(turn[...], summed.reshape(SLOTS, cols).astype(BF16))
-        sendz2[ch] = turned.reshape(NZ, SPOTS, cols).astype(BF16)
-        for other, device in z_peers:
-            send(sendz2.at[ch, other], back.at[ch, z], Z2, ch, device)
-        back[ch, z] = sendz2[ch, z]
-        return 0
-
-    lax.fori_loop(0, CHUNKS, pair_arrives, 0)
-
     load_so.wait()
     sop[...] = dot_tn(place[...], so[...]).astype(BF16)
     dcomb[...] = dot_nt(cot[...], sop[...])
     order = one_hot(functools.partial(column_source, fine), 1, half)
     for k in range(2):
         tokq[:, k * half : (k + 1) * half] = dot_nn(tok[:, k * half : (k + 1) * half], order).astype(BF16)
+
+    def add_to_act(grads, span):
+        for j in range(pieces):
+            part = slice(j * TILE, (j + 1) * TILE)
+            act[:, part] += dot_nt(grads, wout[part, span])
+
+    def rows_arrive(span, k):
+        arrived(rows.at[pl.ds(0, 2 * SPOTS - 1), :, span], W1, k)
+        add_to_act(rows[:, :, span].reshape(2 * SLOTS, span.size), span)
+
+    thrice((rows_arrive, whole_span))
+    for k in range(3):
+        span = mixed_span(k)
+        arrived(recvm.at[pl.ds(0, NZ - 1), :, span], M1, k)
+    add_to_act(dot_tn(swap[...], recvm[:, :, mixed].reshape(2 * SLOTS, mixed.size)).astype(BF16), mixed)
+    rows_arrive(tail, 3)
+    dpre[...] = (act[...] * gate[...]).astype(BF16)
+
+    def rows_back(span, k):
+        part = dot_nt(dpre[...], win[span, :])
+        sendw2[:, :, span] = part.reshape(2 * SPOTS, NZ, span.size).astype(BF16)
+        for _, other, device in w_peers:
+            send(sendw2.at[other, :, span], recvw2.at[me, :, span], W2, k, device)
+        recvw2[me, :, span] = sendw2[me, :, span]
+
+    def rows_back_mixed(span, k):
+        part = dot_nt(dpre[...], win[span, :]).astype(BF16)
+        sendm2[:, :, span] = dot_nn(swap[...], part).reshape(NZ, 2 * SPOTS, span.size).astype(BF16)
+        for other, device in z_peers:
+            send(sendm2.at[other, :, span], recvm2.at[z, :, span], M2, k, device)
+        recvm2[z, :, span] = sendm2[z, :, span]
+
+    rows_back(whole_span(0), 0)
+    thrice((rows_back_mixed, mixed_span))
+    rows_back(whole_span(1), 1)
+    rows_back(whole_span(2), 2)
+    rows_back(tail, 3)
+
+    def dwin_part(k, _):
+        span = aligned(k * TILE, TILE)
+        for j in range(pieces):
+            part = slice(j * TILE, (j + 1) * TILE)
+            dwin_o[span, part] = dot_tn(eiq[:, span], dpre[:, part]).astype(BF16)
+        return 0
+
+    lax.fori_loop(0, wide // TILE, dwin_part, 0)
     ddisp[...] = jnp.zeros_like(ddisp)
 
-    def z_arrives_back(ch, _):
-        arrived(back.at[ch, pl.ds(0, NZ - 1)], Z2, ch)
-        ddisp[...] += dot_nt(tok[:, aligned(ch * cols, cols)], back[ch].reshape(SLOTS, cols))
-        return 0
-
-    lax.fori_loop(0, CHUNKS, z_arrives_back, 0)
+    def m_arrives_back(span, k):
+        arrived(recvm2.at[pl.ds(0, NZ - 1), :, span], M2, k)
+        swapped = dot_tn(swap[...], recvm2[:, :, span].reshape(2 * SLOTS, span.size))
+        sendw2[:, :, span] = swapped.reshape(2 * SPOTS, NZ, span.size).astype(BF16)
+        for _, other, device in w_peers:
+            send(sendw2.at[other, :, span], recvw2.at[me, :, span], V2, k, device)
+        recvw2[me, :, span] = sendw2[me, :, span]
+
+    def pair_sum(span):
+        summed = recvw2[0:SPOTS, :, span].astype(F32) + recvw2[SPOTS : 2 * SPOTS, :, span].astype(F32)
+        turned = dot_tn(turn[...], summed.reshape(SLOTS, span.size).astype(BF16))
+        return turned.reshape(NZ, SPOTS, span.size).astype(BF16)
+
+    def pair_arrives(span, k):
+        arrived(recvw2.at[pl.ds(0, 2 * SPOTS - 1), :, span], W2, k)
+        sendz2[:, :, span] = pair_sum(span)
+        for other, device in z_peers:
+            send(sendz2.at[other, :, span], back.at[z, :, span], Z2, k, device)
+        back[z, :, span] = sendz2[z, :, span]
+
+    thrice((pair_arrives, whole_span), (m_arrives_back, mixed_span))
+    pair_arrives(tail, 3)
+
+    def z_arrives_back(span, k):
+        arrived(back.at[pl.ds(0, NZ - 1), :, span], Z2, k)
+        ddisp[...] += dot_nt(tok[:, span], back[:, :, span].reshape(SLOTS, span.size))
+
+    def v_arrives_back(span, k):
+        arrived(recvw2.at[pl.ds(0, 2 * SPOTS - 1), :, span], V2, k)
+        back[:, :, span] = pair_sum(span)
+
+    thrice((z_arrives_back, whole_span))
+    thrice((v_arrives_back, mixed_span))
+    ddisp[...] += dot_nt(tok[:, mixed], back[:, :, mixed].reshape(SLOTS, mixed.size))
+    z_arrives_back(tail, 3)
 
     d_disp = ddisp[...]
     d_comb = dcomb[...]
@@ -275,14 +353,14 @@
 
     dispatch_b = disp[...].astype(BF16)
 
-    def d_tokens(ch, _):
-        span = aligned(ch * cols, cols)
+    def d_tokens(k, _):
+        span = aligned(k * TILE, TILE)
         dtok_o[:, span] = (
-            dot_nn(dispatch_b, back[ch].reshape(SLOTS, cols)) + dot_nt(dlog[...], phip[span, :])
+            dot_nn(dispatch_b, back[:, :, span].reshape(SLOTS, TILE)) + dot_nt(dlog[...], phip[span, :])
         ).astype(BF16)
         return 0
 
-    lax.fori_loop(0, CHUNKS, d_tokens, 0)
+    lax.fori_loop(0, wide // TILE, d_tokens, 0)
 
     arrived(recva.at[pl.ds(0, 2 * SPOTS - 1)], SW, 0)
     summed = recva[0].astype(F32)
@@ -300,23 +378,29 @@
         total = total + recvb[k]
     dphi_o[...] = total[0:fine, :]
 
-    def sent(ch, _):
-        left(sendz.at[ch, pl.ds(0, NZ - 1)], Z1, ch)
-        left(rows.at[ch, pl.ds(0, 2 * SPOTS - 1)], W1, ch)
-        left(sendw2.at[ch, pl.ds(0, 2 * SPOTS - 1)], W2, ch)
-        left(sendz2.at[ch, pl.ds(0, NZ - 1)], Z2, ch)
-        return 0
-
-    lax.fori_loop(0, CHUNKS, sent, 0)
+    def sent(span, k):
+        left(sendz.at[pl.ds(0, NZ - 1), :, span], Z1, k)
+        left(rows.at[pl.ds(0, 2 * SPOTS - 1), :, span], W1, k)
+        left(sendw2.at[pl.ds(0, 2 * SPOTS - 1), :, span], W2, k)
+        left(sendz2.at[pl.ds(0, NZ - 1), :, span], Z2, k)
+
+    def sent_mixed(span, k):
+        left(rows.at[pl.ds(0, 2 * SPOTS - 1), :, span], V1, k)
+        left(sendm.at[pl.ds(0, NZ - 1), :, span], M1, k)
+        left(sendm2.at[pl.ds(0, NZ - 1), :, span], M2, k)
+        left(recvw2.at[pl.ds(0, 2 * SPOTS - 1), :, span], V2, k)
+
+    thrice((sent, whole_span), (sent_mixed, mixed_span))
+    sent(tail, 3)
     left(senda.at[pl.ds(0, 2 * SPOTS - 1)], SW, 0)
     left(sendb.at[pl.ds(0, NZ - 1)], SZ, 0)
 
 
 def write_out(dtok_i, dphi_i, dwin_i, dtok_o, dphi_o, dwin_o, sem):
-    copies = [
-        pltpu.make_async_copy(src, dst, sem.at[k])
-        for k, (src, dst) in enumerate([(dwin_i, dwin_o), (dtok_i, dtok_o), (dphi_i, dphi_o)])
-    ]
+    copies = [(dtok_i, dtok_o), (dphi_i, dphi_o)]
+    n = dwin_i.shape[0] // 4
+    copies += [(dwin_i.at[pl.ds(k * n, n)], dwin_o.at[pl.ds(k * n, n)]) for k in range(4)]
+    copies = [pltpu.make_async_copy(src, dst, sem.at[k]) for k, (src, dst) in enumerate(copies)]
     for copy in copies:
         copy.start()
     for copy in copies:
@@ -325,7 +409,6 @@
 
 def per_device(tokens, slot_params, slot_outputs, expert_inputs, w_in, w_out, cotangent):
     images, (m, wide), slots, hid = 2 * SLOTS, tokens.shape[1:], SLOTS, w_in.shape[2]
-    cols = wide // CHUNKS
     fine = wide // images
     vmem = pltpu.VMEM
     scratch = [
@@ -335,18 +418,20 @@
         vmem((images, hid), F32), vmem((images, hid), F32),
         vmem((images, hid), BF16), vmem((m, slots), F32), vmem((m, slots), F32), vmem((m, slots), F32),
         vmem((slots, slots), BF16), vmem((slots, slots), BF16), vmem((images, images), BF16),
+        vmem((images, images), BF16), vmem((slots, m), BF16),
     ]
-    by_z = vmem((CHUNKS, NZ, SPOTS, cols), BF16)
-    by_spot = vmem((CHUNKS, SPOTS, NZ, cols), BF16)
-    by_device = vmem((CHUNKS, 2 * SPOTS, NZ, cols), BF16)
+    by_z = vmem((NZ, SPOTS, wide), BF16)
+    by_spot = vmem((SPOTS, NZ, wide), BF16)
+    by_device = vmem((2 * SPOTS, NZ, wide), BF16)
     scratch += [by_z, by_z, by_spot, by_device, by_device, by_device, by_z, by_z]
+    scratch += [vmem((NZ, 2 * SPOTS, wide), BF16)] * 4
     scratch += [
-        vmem((m, slots), F32), vmem((m, slots), BF16),
+        vmem((slots, m), BF16), vmem((m, slots), F32), vmem((m, slots), BF16),
         vmem((2 * SPOTS, NZ * fine, slots), BF16), vmem((2 * SPOTS, NZ * fine, slots), BF16),
         vmem((NZ, 8, slots), F32), vmem((NZ, 8, slots), F32),
     ]
     sems = pltpu.SemaphoreType.DMA
-    scratch += [sems((6, CHUNKS)), sems((6, CHUNKS)), sems((7,))]
+    scratch += [sems((10, 4)), sems((10, 4)), sems((7,))]
     hbm = pl.BlockSpec(memory_space=pl.ANY)
     held = pl.BlockSpec(memory_space=pltpu.VMEM)
     shapes = [
@@ -368,7 +453,7 @@
         out_shape=shapes,
         in_specs=[hbm] * 3,
         out_specs=[hbm] * 3,
-        scratch_shapes=[sems((3,))],
+        scratch_shapes=[sems((6,))],
         compiler_params=pltpu.CompilerParams(vmem_limit_bytes=2**20),
     )(*[pltpu.with_memory_space_constraint(result, pltpu.VMEM) for result in results])
     return (d_tokens[None], d_phi, d_first[None])

time: 55.8 us -> 53.7 us (0.962)
  Pallas kernels: 55.1 us -> 53 us
    pallas_call x1, Pallas kernels: 53.1 us -> 51 us  [per_device(): pl.pallas_call(kernel, out_shape=[pltpu.VMEM(shape.shape, shape.dtype) fo...]
where the time goes in v4:
time: 53.7 us; the launch traced here: 53.6 us
  Pallas kernels  53 us (99%)
  between operations  0.64 us (1%)
    pallas_call x1, Pallas kernels, per_device(): pl.pallas_call(kernel, out_shape=[pltpu.VMEM(shape.shape, shape.dtype) fo...  51 us
    pallas_call x1, Pallas kernels, per_device(): pl.pallas_call(write_out, out_shape=shapes, in_specs=[hbm] * 3, out_specs...  1.97 us

profile of v4, /device:TPU:1, one launch (start us, length us, event | category | flops | bytes accessed | tf_op | source)
XLA Modules:
  0.0 53.6 jit_solution(17606383497689747744)
XLA Ops:
  0.6 51.0 %shard_map.94 = (bf16[256,1280]{1,0:T(8,128)(2,1)S(1)}, f32[5,128]{1,0:T(8,128)S(1)}, bf16[1280,1280]{1,0:T(8,128)(2,1)S(1)}) custom-call(bf16[256,1280]{1,0:T(8,128)(2,1)} %bitcast.10, bf16[1280,128]{1,0:T(8,128)(2,1)} %phi_h.1, bf16[128,1280]{1,0:T(8,128)(2,1)} %bitcast.13, bf16[256,1280]{1,0:T(8,128)(2,1)} %bitcast.11, bf16[1280,1280]{1,0:T(8,128)(2,1)} %bitcast.8, ...), custom_call_target="tpu_custom_call" | custom-call | tf_op jit(solution)/shard_map/pallas_call | solution.py:443
  51.7 2.0 %shard_map.95 = (bf16[256,1280]{1,0:T(8,128)(2,1)}, f32[5,128]{1,0:T(8,128)}, bf16[1280,1280]{1,0:T(8,128)(2,1)}) custom-call(bf16[256,1280]{1,0:T(8,128)(2,1)S(1)} %get-tuple-element.9.dtok_i, f32[5,128]{1,0:T(8,128)S(1)} %get-tuple-element.10.dphi_i, bf16[1280,1280]{1,0:T(8,128)(2,1)S(1)} %get-tuple-element.11.dwin_i), custom_call_target="tpu_custom_call" | custom-call | tf_op jit(solution)/shard_map/pallas_call | solution.py:451

commit v5 on v4

--- a/solution.py
+++ b/solution.py
@@ -285,8 +285,8 @@
         recvm2[z, :, span] = sendm2[z, :, span]
 
     rows_back(whole_span(0), 0)
+    rows_back(whole_span(1), 1)
     thrice((rows_back_mixed, mixed_span))
-    rows_back(whole_span(1), 1)
     rows_back(whole_span(2), 2)
     rows_back(tail, 3)
 
@@ -361,6 +361,21 @@
         return 0
 
     lax.fori_loop(0, wide // TILE, d_tokens, 0)
+
+    def sent(span, k):
+        left(sendz.at[pl.ds(0, NZ - 1), :, span], Z1, k)
+        left(rows.at[pl.ds(0, 2 * SPOTS - 1), :, span], W1, k)
+        left(sendw2.at[pl.ds(0, 2 * SPOTS - 1), :, span], W2, k)
+        left(sendz2.at[pl.ds(0, NZ - 1), :, span], Z2, k)
+
+    def sent_mixed(span, k):
+        left(rows.at[pl.ds(0, 2 * SPOTS - 1), :, span], V1, k)
+        left(sendm.at[pl.ds(0, NZ - 1), :, span], M1, k)
+        left(sendm2.at[pl.ds(0, NZ - 1), :, span], M2, k)
+        left(recvw2.at[pl.ds(0, 2 * SPOTS - 1), :, span], V2, k)
+
+    thrice((sent, whole_span), (sent_mixed, mixed_span))
+    sent(tail, 3)
 
     arrived(recva.at[pl.ds(0, 2 * SPOTS - 1)], SW, 0)
     summed = recva[0].astype(F32)
@@ -372,27 +387,13 @@
     for other, device in z_peers:
         send(sendb.at[other], recvb.at[z], SZ, 0, device)
     recvb[z] = sendb[z]
+    left(senda.at[pl.ds(0, 2 * SPOTS - 1)], SW, 0)
     arrived(recvb.at[pl.ds(0, NZ - 1)], SZ, 0)
     total = recvb[0]
     for k in range(1, NZ):
         total = total + recvb[k]
     dphi_o[...] = total[0:fine, :]
 
-    def sent(span, k):
-        left(sendz.at[pl.ds(0, NZ - 1), :, span], Z1, k)
-        left(rows.at[pl.ds(0, 2 * SPOTS - 1), :, span], W1, k)
-        left(sendw2.at[pl.ds(0, 2 * SPOTS - 1), :, span], W2, k)
-        left(sendz2.at[pl.ds(0, NZ - 1), :, span], Z2, k)
-
-    def sent_mixed(span, k):
-        left(rows.at[pl.ds(0, 2 * SPOTS - 1), :, span], V1, k)
-        left(sendm.at[pl.ds(0, NZ - 1), :, span], M1, k)
-        left(sendm2.at[pl.ds(0, NZ - 1), :, span], M2, k)
-        left(recvw2.at[pl.ds(0, 2 * SPOTS - 1), :, span], V2, k)
-
-    thrice((sent, whole_span), (sent_mixed, mixed_span))
-    sent(tail, 3)
-    left(senda.at[pl.ds(0, 2 * SPOTS - 1)], SW, 0)
     left(sendb.at[pl.ds(0, NZ - 1)], SZ, 0)
 
 

time: 53.7 us -> 53.7 us (level)
  no operation moved by 1% of the time
where the time goes in v5:
time: 53.7 us; the launch traced here: 53.6 us
  Pallas kernels  52.9 us (99%)
  between operations  0.64 us (1%)
    pallas_call x1, Pallas kernels, per_device(): pl.pallas_call(kernel, out_shape=[pltpu.VMEM(shape.shape, shape.dtype) fo...  51 us
    pallas_call x1, Pallas kernels, per_device(): pl.pallas_call(write_out, out_shape=shapes, in_specs=[hbm] * 3, out_specs...  1.97 us

profile of v5, /device:TPU:1, one launch (start us, length us, event | category | flops | bytes accessed | tf_op | source)
XLA Modules:
  0.0 53.6 jit_solution(14833197637359969482)
XLA Ops:
  0.6 51.0 %shard_map.94 = (bf16[256,1280]{1,0:T(8,128)(2,1)S(1)}, f32[5,128]{1,0:T(8,128)S(1)}, bf16[1280,1280]{1,0:T(8,128)(2,1)S(1)}) custom-call(bf16[256,1280]{1,0:T(8,128)(2,1)} %bitcast.10, bf16[1280,128]{1,0:T(8,128)(2,1)} %phi_h.1, bf16[128,1280]{1,0:T(8,128)(2,1)} %bitcast.13, bf16[256,1280]{1,0:T(8,128)(2,1)} %bitcast.11, bf16[1280,1280]{1,0:T(8,128)(2,1)} %bitcast.8, ...), custom_call_target="tpu_custom_call" | custom-call | tf_op jit(solution)/shard_map/pallas_call | solution.py:444
  51.6 2.0 %shard_map.95 = (bf16[256,1280]{1,0:T(8,128)(2,1)}, f32[5,128]{1,0:T(8,128)}, bf16[1280,1280]{1,0:T(8,128)(2,1)}) custom-call(bf16[256,1280]{1,0:T(8,128)(2,1)S(1)} %get-tuple-element.9.dtok_i, f32[5,128]{1,0:T(8,128)S(1)} %get-tuple-element.10.dphi_i, bf16[1280,1280]{1,0:T(8,128)(2,1)S(1)} %get-tuple-element.11.dwin_i), custom_call_target="tpu_custom_call" | custom-call | tf_op jit(solution)/shard_map/pallas_call | solution.py:452
